TPU v7x, 32 devices: a whole 2x2x4 slice. The times are simulated.
32 devices in a mesh: gx: 4 (over z), gy: 4 (over x, core), gz: 2 (over y).
Axes of the slice: x: 2, y: 2, z: 4, core: 2. Of those that a mesh axis runs over, the one named last changes fastest.
Arguments:
- coefficients: bfloat16 [8, 16, 4, 512, 128], P('gx', 'gy', 'gz'), may hold values from -6 to 6
- level_weights: bfloat16 [4, 2, 2, 512, 512], replicated, may hold values from -0.125 to 0.125
- coupling: bfloat16 [6, 512, 512], replicated, may hold values from -0.109375 to 0.109375
- positions: float32 [3, 262144], P(None, ('gx', 'gy', 'gz')), may hold values from -1 to 1
- block_leaf: int32 [2048], P(('gx', 'gy', 'gz')), may hold values from 0 to 15
- block_count: int32 [2048], P(('gx', 'gy', 'gz')), may hold values from 1 to 128
Outputs:
- samples: bfloat16 [262144, 128], P(('gx', 'gy', 'gz'))
Inputs may be any that keep to these rules, and one draw needn't show every extreme that they name: `block_leaf`: each block names one of the 16 leaves of the device that holds the block.
All inputs are finite; a program needn't handle non-finite values.
Results may differ from a plain program's by a relative error of at most 0.015.
Values may be sent and summed in bfloat16 or wider, within the bound.
A program may use at most 128 MiB of HBM per device.

v0:
```python
import functools
import math

import jax
import jax.numpy as jnp
from jax import lax
from jax.experimental import pallas as pl
from jax.experimental.pallas import tpu as pltpu
from jax.sharding import PartitionSpec as P

PTS = 8
ROWS = 128
MESH = pl.DeviceIdType.MESH
NT = (((1,), (1,)), ((), ()))


def flat(value):
    return value.reshape(-1, value.shape[-1])


def grid_kernel(sizes, x_ref, w_hbm, k_hbm, out_ref, w_ref, k_ref, src, xin, mid, got, pad, res,
                w_sem, k_sem, fs_sem, fr_sem, ms_sem, mr_sem, hs_sem, hr_sem, zs_sem, zr_sem, bs_sem, br_sem):
    nx, ny, nz = sizes
    lx, ly, lz = x_ref.shape[:3]
    groups = 2 * nx
    per = x_ref.shape[-1] // 2 // groups
    gx, gy, gz = lax.axis_index("gx"), lax.axis_index("gy"), lax.axis_index("gz")
    bit = lax.rem(gz, 2)
    base = gz - bit
    me = gx * 2 + bit
    wide_x, wide_z = nx * lx, 2 * lz

    def peer(step):
        other = lax.rem(me + step, groups)
        return other, lax.div(other, 2), lax.rem(other, 2)

    def when(cond):
        return pl.when(cond)

    for level in range(4):
        pltpu.make_async_copy(w_hbm.at[level], w_ref.at[level], w_sem.at[level]).start()
    pltpu.make_async_copy(k_hbm, k_ref, k_sem).start()

    barrier = pltpu.get_barrier_semaphore()
    for step in range(1, groups):
        _, px, pz = peer(step)
        pl.semaphore_signal(barrier, inc=1, device_id=(px, gy, base + pz), device_id_type=MESH)

    @when(gy > 0)
    def _():
        pl.semaphore_signal(barrier, inc=1, device_id=(gx, gy - 1, gz), device_id_type=MESH)

    @when(gy < ny - 1)
    def _():
        pl.semaphore_signal(barrier, inc=1, device_id=(gx, gy + 1, gz), device_id_type=MESH)

    if nz > 2:
        @when(gz > 1)
        def _():
            pl.semaphore_signal(barrier, inc=1, device_id=(gx, gy, gz - 2), device_id_type=MESH)

        @when(gz < nz - 2)
        def _():
            pl.semaphore_signal(barrier, inc=1, device_id=(gx, gy, gz + 2), device_id_type=MESH)

    def turn(t):
        y = lax.rem(3 * t, ly)
        for a in range(lx):
            for b in range(lz):
                block = x_ref[a, y, b].astype(jnp.float32).T
                half = block.shape[0] // 2
                for g in range(groups):
                    both = jnp.concatenate(
                        [block[g * per:(g + 1) * per], block[half + g * per:half + (g + 1) * per]], axis=0
                    )
                    src[g, y, a, b] = both.astype(jnp.bfloat16)
        xin[y, pl.ds(gx * lx, lx), pl.ds(bit * lz, lz)] = src[me, y]

    def forward(t, step):
        y = lax.rem(3 * t, ly)
        other, px, pz = peer(step)
        return pltpu.make_async_remote_copy(
            src_ref=src.at[other, y],
            dst_ref=xin.at[y, pl.ds(gx * lx, lx), pl.ds(bit * lz, lz)],
            send_sem=fs_sem.at[step, y],
            recv_sem=fr_sem.at[step, y],
            device_id=(px, gy, base + pz),
            device_id_type=MESH,
        )

    turn(0)
    def one(cond):
        return jnp.where(cond, 1, 0).astype(jnp.int32)

    peers = groups - 1 + one(gy > 0) + one(gy < ny - 1)
    if nz > 2:
        peers = peers + one(gz > 1) + one(gz < nz - 2)
    pl.semaphore_wait(barrier, peers)

    @pl.loop(0, ly)
    def _(t):
        @when(t > 0)
        def _():
            turn(t)
        for step in range(1, groups):
            forward(t, step).start()

    pad[:, 0] = jnp.zeros_like(pad[:, 0])
    pad[:, wide_x + 1] = jnp.zeros_like(pad[:, 0])

    def no_plane(z):
        for y in range(1, ly + 1):
            pad[y, 1:wide_x + 1, z] = jnp.zeros_like(pad[0, 1:wide_x + 1, 0])

    if nz > 2:
        when(gz < 2)(lambda: no_plane(0))
        when(gz >= nz - 2)(lambda: no_plane(wide_z + 1))
    else:
        no_plane(0)
        no_plane(wide_z + 1)

    @when(gy == 0)
    def _():
        pad[0, 1:wide_x + 1] = jnp.zeros_like(pad[0, 1:wide_x + 1])

    @when(gy == ny - 1)
    def _():
        pad[ly + 1, 1:wide_x + 1] = jnp.zeros_like(pad[0, 1:wide_x + 1])

    def mixed(level, own, other):
        shape = own.shape
        a, b = flat(own), flat(other)
        dot = functools.partial(lax.dot_general, dimension_numbers=NT, preferred_element_type=jnp.float32)
        straight = dot(a, w_ref[level, 0, 0]) + dot(b, w_ref[level, 1, 0])
        cross = dot(a, w_ref[level, 0, 1]) + dot(b, w_ref[level, 1, 1])
        straight = straight.reshape(-1, 2, per, shape[-1])
        cross = cross.reshape(-1, 2, per, shape[-1])
        real = straight[:, 0] - cross[:, 1]
        imag = straight[:, 1] + cross[:, 0]
        return jnp.stack([real, imag], axis=1).reshape(shape).astype(jnp.bfloat16)

    def flip(value, dim, width):
        pieces = []
        for at in range(0, value.shape[dim], 2 * width):
            pieces.append(lax.slice_in_dim(value, at + width, at + 2 * width, axis=dim))
            pieces.append(lax.slice_in_dim(value, at, at + width, axis=dim))
        return jnp.concatenate(pieces, axis=dim)

    def to_core(y):
        return pltpu.make_async_remote_copy(
            src_ref=mid.at[y], dst_ref=got.at[y], send_sem=ms_sem.at[y], recv_sem=mr_sem.at[y],
            device_id=(gx, gy + 1 - 2 * lax.rem(gy, 2), gz), device_id_type=MESH,
        )

    inner = (pl.ds(1, wide_x), pl.ds(1, wide_z))

    def halo(up):
        return pltpu.make_async_remote_copy(
            src_ref=pad.at[(ly if up else 1,) + inner],
            dst_ref=pad.at[(0 if up else ly + 1,) + inner],
            send_sem=hs_sem.at[int(up)], recv_sem=hr_sem.at[int(up)],
            device_id=(gx, gy + 1 if up else gy - 1, gz), device_id_type=MESH,
        )

    def halo_z(up):
        rows = pl.ds(1, ly), pl.ds(1, wide_x)
        return pltpu.make_async_remote_copy(
            src_ref=pad.at[rows + (wide_z if up else 1,)],
            dst_ref=pad.at[rows + (0 if up else wide_z + 1,)],
            send_sem=zs_sem.at[int(up)], recv_sem=zr_sem.at[int(up)],
            device_id=(gx, gy, gz + 2 if up else gz - 2), device_id_type=MESH,
        )

    for level in range(4):
        pltpu.make_async_copy(w_hbm.at[level], w_ref.at[level], w_sem.at[level]).wait()

    @pl.loop(0, ly + 1)
    def _(t):
        @when(t < ly)
        def _():
            y = lax.rem(3 * t, ly)
            for step in range(1, groups):
                forward(t, step).wait_recv()
            own = xin[y]
            own = mixed(0, own, flip(own, 0, lx))
            mid[y] = mixed(1, own, flip(own, 0, 2 * lx))
            to_core(y).start()

        @when(t > 0)
        def _():
            y = lax.rem(3 * (t - 1), ly)
            to_core(y).wait_recv()
            own = mixed(2, mid[y], got[y])
            pad[y + 1, 1:wide_x + 1, 1:wide_z + 1] = mixed(3, own, flip(own, 1, lz))

            @when(jnp.logical_and(y == 0, gy > 0))
            def _():
                halo(False).start()

            @when(jnp.logical_and(y == ly - 1, gy < ny - 1))
            def _():
                halo(True).start()

    if nz > 2:
        @when(gz < nz - 2)
        def _():
            halo_z(True).start()

        @when(gz > 1)
        def _():
            halo_z(False).start()

        @when(gz > 1)
        def _():
            halo_z(True).wait_recv()

        @when(gz < nz - 2)
        def _():
            halo_z(False).wait_recv()

    pltpu.make_async_copy(k_hbm, k_ref, k_sem).wait()

    @when(gy < ny - 1)
    def _():
        halo(False).wait_recv()

    @when(gy > 0)
    def _():
        halo(True).wait_recv()

    def back(y, step):
        other, px, pz = peer(step)
        return pltpu.make_async_remote_copy(
            src_ref=res.at[y, pl.ds(px * lx, lx), pl.ds(pz * lz, lz)],
            dst_ref=out_ref.at[me, y],
            send_sem=bs_sem.at[step, y], recv_sem=br_sem.at[step, y],
            device_id=(px, gy, base + pz), device_id_type=MESH,
        )

    @pl.loop(0, ly)
    def _(t):
        y = ly - 1 - t
        xs, zs = pl.ds(1, wide_x), pl.ds(1, wide_z)
        here = pad[y + 1, xs, zs]
        total = flat(here).astype(jnp.float32)
        places = (
            (y + 1, pl.ds(0, wide_x), zs), (y + 1, pl.ds(2, wide_x), zs),
            (y, xs, zs), (y + 2, xs, zs),
            (y + 1, xs, pl.ds(0, wide_z)), (y + 1, xs, pl.ds(2, wide_z)),
        )
        for d, place in enumerate(places):
            total = total + lax.dot_general(flat(pad[place]), k_ref[d], NT, preferred_element_type=jnp.float32)
        res[y] = total.astype(jnp.bfloat16).reshape(here.shape)
        for step in range(1, groups):
            back(y, step).start()
        out_ref[me, y] = res[y, pl.ds(gx * lx, lx), pl.ds(bit * lz, lz)]

    @pl.loop(0, ly)
    def _(t):
        for step in range(1, groups):
            forward(t, step).wait_send()
            back(t, step).wait_send()
            back(t, step).wait_recv()
        to_core(t).wait_send()

    @when(gy > 0)
    def _():
        halo(False).wait_send()

    @when(gy < ny - 1)
    def _():
        halo(True).wait_send()

    if nz > 2:
        @when(gz < nz - 2)
        def _():
            halo_z(True).wait_send()

        @when(gz > 1)
        def _():
            halo_z(False).wait_send()


def grid_of(coefficients, level_weights, coupling, sizes):
    nx, ny, nz = sizes
    lx, ly, lz, cheb, cols = coefficients.shape
    groups = 2 * nx
    rows = cols // groups
    bf = jnp.bfloat16
    plane = (nx * lx, 2 * lz, rows, cheb)
    dma = pltpu.SemaphoreType.DMA
    anywhere = pl.BlockSpec(memory_space=pl.ANY)
    vmem = pl.BlockSpec(memory_space=pltpu.VMEM)
    return pl.pallas_call(
        functools.partial(grid_kernel, sizes),
        out_shape=jax.ShapeDtypeStruct((groups, ly, lx, lz, rows, cheb), bf),
        in_specs=[vmem, anywhere, anywhere],
        out_specs=vmem,
        scratch_shapes=[
            pltpu.VMEM(level_weights.shape, bf),
            pltpu.VMEM(coupling.shape, bf),
            pltpu.VMEM((groups, ly, lx, lz, rows, cheb), bf),
            pltpu.VMEM((ly,) + plane, bf),
            pltpu.VMEM((ly,) + plane, bf),
            pltpu.VMEM((ly,) + plane, bf),
            pltpu.VMEM((ly + 2, nx * lx + 2, 2 * lz + 2, rows, cheb), bf),
            pltpu.VMEM((ly,) + plane, bf),
            dma((4,)), dma,
            dma((groups, ly)), dma((groups, ly)),
            dma((ly,)), dma((ly,)),
            dma((2,)), dma((2,)), dma((2,)), dma((2,)),
            dma((groups, ly)), dma((groups, ly)),
        ],
        compiler_params=pltpu.CompilerParams(
            collective_id=0, has_side_effects=True, vmem_limit_bytes=56 << 20
        ),
    )(coefficients, level_weights, coupling)


def basis_of(coords):
    nodes = [math.cos(math.pi * (2 * j + 1) / (2 * PTS)) for j in range(PTS)]
    diffs = [coords - jnp.float32(node) for node in nodes]
    basis = []
    for j in range(PTS):
        scale = 1.0
        term = None
        for m in range(PTS):
            if m != j:
                scale *= nodes[j] - nodes[m]
                term = diffs[m] if term is None else term * diffs[m]
        basis.append(term * jnp.float32(1.0 / scale))
    return basis


def sample_kernel(leaf_ref, count_ref, pos_ref, grid_ref, out_ref, held):
    groups, ly, lx, lz, rows, cheb = grid_ref.shape
    per = rows // 2
    for a in range(lx):
        for y in range(ly):
            for b in range(lz):
                parts = [grid_ref[g, y, a, b].astype(jnp.float32) for g in range(groups)]
                whole = [part[:per] for part in parts] + [part[per:] for part in parts]
                held[(a * ly + y) * lz + b] = jnp.concatenate(whole, axis=0).astype(jnp.bfloat16)

    @pl.loop(0, leaf_ref.shape[0])
    def _(i):
        start = pl.multiple_of(i * ROWS, ROWS)
        along = [basis_of(pos_ref[d:d + 1, pl.ds(start, ROWS)]) for d in range(3)]
        last = jnp.concatenate(along[2], axis=0)
        tiles = []
        for jx in range(PTS):
            for jy in range(PTS):
                tiles.append((along[0][jx] * along[1][jy]) * last)
        weights = jnp.concatenate(tiles, axis=0).astype(jnp.bfloat16)
        values = jnp.dot(held[leaf_ref[i]], weights, preferred_element_type=jnp.float32)
        values = values.T
        live = lax.broadcasted_iota(jnp.int32, values.shape, 0) < count_ref[i]
        out_ref[pl.ds(start, ROWS), :] = jnp.where(live, values, 0.0).astype(jnp.bfloat16)


def samples_of(grid, positions, block_leaf, block_count):
    groups, ly, lx, lz, rows, cheb = grid.shape
    smem = pl.BlockSpec(memory_space=pltpu.SMEM)
    vmem = pl.BlockSpec(memory_space=pltpu.VMEM)
    return pl.pallas_call(
        sample_kernel,
        out_shape=jax.ShapeDtypeStruct((positions.shape[1], groups * rows), jnp.bfloat16),
        in_specs=[smem, smem, vmem, vmem],
        out_specs=vmem,
        scratch_shapes=[pltpu.VMEM((lx * ly * lz, groups * rows, cheb), jnp.bfloat16)],
        compiler_params=pltpu.CompilerParams(vmem_limit_bytes=40 << 20),
    )(block_leaf, block_count, positions, grid)


def local(sizes, coefficients, level_weights, coupling, positions, block_leaf, block_count):
    grid = grid_of(coefficients, level_weights, coupling, sizes)
    return samples_of(grid, positions, block_leaf, block_count)


def solution(mesh):
    sizes = (mesh.shape["gx"], mesh.shape["gy"], mesh.shape["gz"])
    placed = (
        P("gx", "gy", "gz", None, None),
        P(),
        P(),
        P(None, ("gx", "gy", "gz")),
        P(("gx", "gy", "gz")),
        P(("gx", "gy", "gz")),
    )
    return jax.shard_map(
        functools.partial(local, sizes), mesh=mesh, in_specs=placed,
        out_specs=P(("gx", "gy", "gz"), None), check_vma=False,
    )
```

profile of v0, /device:TPU:30, one launch (start us, length us, event | category | flops | bytes accessed | tf_op | source)
XLA Modules:
  0.0 131.0 jit_solution(12958827383049064592)
XLA Ops:
  0.0 0.0 copy-start.3
  0.0 0.0 copy-start.2
  0.0 0.0 copy-start.1
  0.0 109.2 %shard_map.64.grid_ref = bf16[8,4,2,2,16,512]{5,4,3,2,1,0:T(8,128)(2,1)} custom-call(bf16[2,4,2,512,128]{4,3,2,1,0:T(8,128)(2,1)} %x_ref.1, bf16[4,2,2,512,512]{4,3,2,1,0:T(8,128)(2,1)} %w_hbm.1, bf16[6,512,512]{2,1,0:T(8,128)(2,1)} %k_hbm.1), custom_call_target="tpu_custom_call" | custom-call | tf_op jit(solution)/shard_map/pallas_call | solution.py:294
  109.2 0.0 copy-done.3
  109.2 0.0 copy-done.2
  109.3 0.0 copy-done.1
  109.3 0.0 copy-start
  109.3 1.6 %copy-done = bf16[8,4,2,2,16,512]{5,4,3,2,1,0:T(8,128)(2,1)S(1)} copy-done((bf16[8,4,2,2,16,512]{5,4,3,2,1,0:T(8,128)(2,1)S(1)}, bf16[8,4,2,2,16,512]{5,4,3,2,1,0:T(8,128)(2,1)}, u32[]{:S(2)}) %copy-start) | copy-done | bytes 2097176
  110.9 20.2 %shard_map.65 = bf16[8192,128]{1,0:T(8,128)(2,1)} custom-call(s32[64]{0:T(128)S(1)} %copy-done.2, s32[64]{0:T(128)S(1)} %copy-done.3, f32[3,8192]{1,0:T(4,128)S(1)} %copy-done.1, bf16[8,4,2,2,16,512]{5,4,3,2,1,0:T(8,128)(2,1)S(1)} %copy-done), custom_call_target="tpu_custom_call" | custom-call | tf_op jit(solution)/shard_map/pallas_call | solution.py:365
Async XLA Ops:
  0.0 109.2 %copy-start.3 = (s32[64]{0:T(128)S(1)}, s32[64]{0:T(128)}, u32[]{:S(2)}) copy-start(s32[64]{0:T(128)} %count_ref.1) | copy-start | bytes 772
  0.0 109.2 %copy-start.2 = (s32[64]{0:T(128)S(1)}, s32[64]{0:T(128)}, u32[]{:S(2)}) copy-start(s32[64]{0:T(128)} %leaf_ref.1) | copy-start | bytes 772
  0.0 109.3 %copy-start.1 = (f32[3,8192]{1,0:T(4,128)S(1)}, f32[3,8192]{1,0:T(4,128)}, u32[]{:S(2)}) copy-start(f32[3,8192]{1,0:T(4,128)} %pos_ref.1) | copy-start | bytes 294916
  109.3 1.6 %copy-start = (bf16[8,4,2,2,16,512]{5,4,3,2,1,0:T(8,128)(2,1)S(1)}, bf16[8,4,2,2,16,512]{5,4,3,2,1,0:T(8,128)(2,1)}, u32[]{:S(2)}) copy-start(bf16[8,4,2,2,16,512]{5,4,3,2,1,0:T(8,128)(2,1)} %shard_map.64.grid_ref) | copy-start | bytes 6291460
where the time goes:
time: 131 us
  Pallas kernels  129 us (98%)
  local copies, waits for them, and re-layouts  1.6 us (1%)
    pallas_call x1, Pallas kernels, grid_of(): pl.pallas_call(functools.partial(grid_kernel, sizes), out_shape=jax.Shape...  109 us
    pallas_call x1, Pallas kernels, samples_of(): pl.pallas_call(sample_kernel, out_shape=jax.ShapeDtypeStruct((positions.s...  20.2 us

commit v1 on v0

v1 whole, which is shorter than its diff:
```python
import functools
import math

import jax
import jax.numpy as jnp
from jax import lax
from jax.experimental import pallas as pl
from jax.experimental.pallas import tpu as pltpu
from jax.sharding import PartitionSpec as P

PTS = 8
ROWS = 128
MESH = pl.DeviceIdType.MESH
NT = (((1,), (1,)), ((), ()))


def flat(value):
    return value.reshape(-1, value.shape[-1])


def basis_of(coords):
    nodes = [math.cos(math.pi * (2 * j + 1) / (2 * PTS)) for j in range(PTS)]
    diffs = [coords - jnp.float32(node) for node in nodes]
    basis = []
    for j in range(PTS):
        scale = 1.0
        term = None
        for m in range(PTS):
            if m != j:
                scale *= nodes[j] - nodes[m]
                term = diffs[m] if term is None else term * diffs[m]
        basis.append(term * jnp.float32(1.0 / scale))
    return basis


def grid_kernel(sizes, leaf_ref, count_ref, x_ref, pos_ref, w_hbm, k_hbm, out_ref,
                w_ref, k_ref, src, xin, mid, got, pad, res, home, held, wts,
                w_sem, k_sem, fs_sem, fr_sem, ms_sem, mr_sem, hs_sem, hr_sem, zs_sem, zr_sem, bs_sem, br_sem):
    nx, ny, nz = sizes
    lx, ly, lz = x_ref.shape[:3]
    groups = 2 * nx
    per = x_ref.shape[-1] // 2 // groups
    gx, gy, gz = lax.axis_index("gx"), lax.axis_index("gy"), lax.axis_index("gz")
    bit = lax.rem(gz, 2)
    base = gz - bit
    me = gx * 2 + bit
    wide_x, wide_z = nx * lx, 2 * lz

    def peer(step):
        other = lax.rem(me + step, groups)
        return other, lax.div(other, 2), lax.rem(other, 2)

    def when(cond):
        return pl.when(cond)

    for level in range(4):
        pltpu.make_async_copy(w_hbm.at[level], w_ref.at[level], w_sem.at[level]).start()
    pltpu.make_async_copy(k_hbm, k_ref, k_sem).start()

    barrier = pltpu.get_barrier_semaphore()
    for step in range(1, groups):
        _, px, pz = peer(step)
        pl.semaphore_signal(barrier, inc=1, device_id=(px, gy, base + pz), device_id_type=MESH)

    @when(gy > 0)
    def _():
        pl.semaphore_signal(barrier, inc=1, device_id=(gx, gy - 1, gz), device_id_type=MESH)

    @when(gy < ny - 1)
    def _():
        pl.semaphore_signal(barrier, inc=1, device_id=(gx, gy + 1, gz), device_id_type=MESH)

    if nz > 2:
        @when(gz > 1)
        def _():
            pl.semaphore_signal(barrier, inc=1, device_id=(gx, gy, gz - 2), device_id_type=MESH)

        @when(gz < nz - 2)
        def _():
            pl.semaphore_signal(barrier, inc=1, device_id=(gx, gy, gz + 2), device_id_type=MESH)

    def turn(t):
        y = lax.rem(ly - t, ly)
        for a in range(lx):
            for b in range(lz):
                block = x_ref[a, y, b].astype(jnp.float32).T
                half = block.shape[0] // 2
                for g in range(groups):
                    both = jnp.concatenate(
                        [block[g * per:(g + 1) * per], block[half + g * per:half + (g + 1) * per]], axis=0
                    )
                    src[g, y, a, b] = both.astype(jnp.bfloat16)
        xin[y, pl.ds(gx * lx, lx), pl.ds(bit * lz, lz)] = src[me, y]

    def forward(t, step):
        y = lax.rem(ly - t, ly)
        other, px, pz = peer(step)
        return pltpu.make_async_remote_copy(
            src_ref=src.at[other, y],
            dst_ref=xin.at[y, pl.ds(gx * lx, lx), pl.ds(bit * lz, lz)],
            send_sem=fs_sem.at[step, y],
            recv_sem=fr_sem.at[step, y],
            device_id=(px, gy, base + pz),
            device_id_type=MESH,
        )

    turn(0)
    def one(cond):
        return jnp.where(cond, 1, 0).astype(jnp.int32)

    peers = groups - 1 + one(gy > 0) + one(gy < ny - 1)
    if nz > 2:
        peers = peers + one(gz > 1) + one(gz < nz - 2)
    pl.semaphore_wait(barrier, peers)

    @pl.loop(0, ly)
    def _(t):
        @when(t > 0)
        def _():
            turn(t)
        for step in range(1, groups):
            forward(t, step).start()

    pad[:, 0] = jnp.zeros_like(pad[:, 0])
    pad[:, wide_x + 1] = jnp.zeros_like(pad[:, 0])

    def no_plane(z):
        for y in range(1, ly + 1):
            pad[y, 1:wide_x + 1, z] = jnp.zeros_like(pad[0, 1:wide_x + 1, 0])

    if nz > 2:
        when(gz < 2)(lambda: no_plane(0))
        when(gz >= nz - 2)(lambda: no_plane(wide_z + 1))
    else:
        no_plane(0)
        no_plane(wide_z + 1)

    @when(gy == 0)
    def _():
        pad[0, 1:wide_x + 1] = jnp.zeros_like(pad[0, 1:wide_x + 1])

    @when(gy == ny - 1)
    def _():
        pad[ly + 1, 1:wide_x + 1] = jnp.zeros_like(pad[0, 1:wide_x + 1])

    def mixed(level, own, other):
        shape = own.shape
        a, b = flat(own), flat(other)
        dot = functools.partial(lax.dot_general, dimension_numbers=NT, preferred_element_type=jnp.float32)
        straight = dot(a, w_ref[level, 0, 0]) + dot(b, w_ref[level, 1, 0])
        cross = dot(a, w_ref[level, 0, 1]) + dot(b, w_ref[level, 1, 1])
        straight = straight.reshape(-1, 2, per, shape[-1])
        cross = cross.reshape(-1, 2, per, shape[-1])
        real = straight[:, 0] - cross[:, 1]
        imag = straight[:, 1] + cross[:, 0]
        return jnp.stack([real, imag], axis=1).reshape(shape).astype(jnp.bfloat16)

    def flip(value, dim, width):
        pieces = []
        for at in range(0, value.shape[dim], 2 * width):
            pieces.append(lax.slice_in_dim(value, at + width, at + 2 * width, axis=dim))
            pieces.append(lax.slice_in_dim(value, at, at + width, axis=dim))
        return jnp.concatenate(pieces, axis=dim)

    def to_core(y):
        return pltpu.make_async_remote_copy(
            src_ref=mid.at[y], dst_ref=got.at[y], send_sem=ms_sem.at[y], recv_sem=mr_sem.at[y],
            device_id=(gx, gy + 1 - 2 * lax.rem(gy, 2), gz), device_id_type=MESH,
        )

    inner = (pl.ds(1, wide_x), pl.ds(1, wide_z))

    def halo(up):
        return pltpu.make_async_remote_copy(
            src_ref=pad.at[(ly if up else 1,) + inner],
            dst_ref=pad.at[(0 if up else ly + 1,) + inner],
            send_sem=hs_sem.at[int(up)], recv_sem=hr_sem.at[int(up)],
            device_id=(gx, gy + 1 if up else gy - 1, gz), device_id_type=MESH,
        )

    def halo_z(up):
        rows = pl.ds(1, ly), pl.ds(1, wide_x)
        return pltpu.make_async_remote_copy(
            src_ref=pad.at[rows + (wide_z if up else 1,)],
            dst_ref=pad.at[rows + (0 if up else wide_z + 1,)],
            send_sem=zs_sem.at[int(up)], recv_sem=zr_sem.at[int(up)],
            device_id=(gx, gy, gz + 2 if up else gz - 2), device_id_type=MESH,
        )

    for level in range(4):
        pltpu.make_async_copy(w_hbm.at[level], w_ref.at[level], w_sem.at[level]).wait()

    def back(y, step):
        other, px, pz = peer(step)
        return pltpu.make_async_remote_copy(
            src_ref=res.at[y, pl.ds(px * lx, lx), pl.ds(pz * lz, lz)],
            dst_ref=home.at[me, y],
            send_sem=bs_sem.at[step, y], recv_sem=br_sem.at[step, y],
            device_id=(px, gy, base + pz), device_id_type=MESH,
        )

    def couple(y):
        xs, zs = pl.ds(1, wide_x), pl.ds(1, wide_z)
        here = pad[y + 1, xs, zs]
        total = flat(here).astype(jnp.float32)
        places = (
            (y + 1, pl.ds(0, wide_x), zs), (y + 1, pl.ds(2, wide_x), zs),
            (y, xs, zs), (y + 2, xs, zs),
            (y + 1, xs, pl.ds(0, wide_z)), (y + 1, xs, pl.ds(2, wide_z)),
        )
        for d, place in enumerate(places):
            total = total + lax.dot_general(flat(pad[place]), k_ref[d], NT, preferred_element_type=jnp.float32)
        res[y] = total.astype(jnp.bfloat16).reshape(here.shape)
        for step in range(1, groups):
            back(y, step).start()
        home[me, y] = res[y, pl.ds(gx * lx, lx), pl.ds(bit * lz, lz)]

    def from_above():
        pltpu.make_async_copy(k_hbm, k_ref, k_sem).wait()

        @when(gy < ny - 1)
        def _():
            halo(False).wait_recv()

    early = nz == 2

    @pl.loop(0, ly + 1)
    def _(t):
        @when(t > 0)
        def _():
            y = lax.rem(ly + 1 - t, ly)
            to_core(y).wait_recv()
            own = mixed(2, mid[y], got[y])
            pad[y + 1, 1:wide_x + 1, 1:wide_z + 1] = mixed(3, own, flip(own, 1, lz))

            @when(jnp.logical_and(y == 0, gy > 0))
            def _():
                halo(False).start()

            @when(jnp.logical_and(y == ly - 1, gy < ny - 1))
            def _():
                halo(True).start()

        if early:
            @when(t == ly - 1)
            def _():
                from_above()
                couple(ly - 1)

        @when(t < ly)
        def _():
            y = lax.rem(ly - t, ly)
            for step in range(1, groups):
                forward(t, step).wait_recv()
            own = xin[y]
            own = mixed(0, own, flip(own, 0, lx))
            mid[y] = mixed(1, own, flip(own, 0, 2 * lx))
            to_core(y).start()

    if nz > 2:
        @when(gz < nz - 2)
        def _():
            halo_z(True).start()

        @when(gz > 1)
        def _():
            halo_z(False).start()

        @when(gz > 1)
        def _():
            halo_z(True).wait_recv()

        @when(gz < nz - 2)
        def _():
            halo_z(False).wait_recv()

    if not early:
        from_above()

    @when(gy > 0)
    def _():
        halo(True).wait_recv()

    @pl.loop(1 if early else 0, ly)
    def _(t):
        couple(ly - 1 - t)

    @pl.loop(0, leaf_ref.shape[0])
    def _(i):
        start = pl.multiple_of(i * ROWS, ROWS)
        along = [basis_of(pos_ref[d:d + 1, pl.ds(start, ROWS)]) for d in range(3)]
        last = jnp.concatenate(along[2], axis=0)
        for jx in range(PTS):
            tiles = [(along[0][jx] * along[1][jy]) * last for jy in range(PTS)]
            wts[i, jx * PTS * PTS:(jx + 1) * PTS * PTS] = jnp.concatenate(tiles, axis=0).astype(jnp.bfloat16)

    @pl.loop(0, ly)
    def _(t):
        y = ly - 1 - t
        for step in range(1, groups):
            back(y, step).wait_recv()
        for a in range(lx):
            for b in range(lz):
                parts = [home[g, y, a, b].astype(jnp.float32) for g in range(groups)]
                whole = [part[:per] for part in parts] + [part[per:] for part in parts]
                held[(a * ly + y) * lz + b] = jnp.concatenate(whole, axis=0).astype(jnp.bfloat16)

    @pl.loop(0, leaf_ref.shape[0] // 4)
    def _(k):
        for j in range(4):
            i = k * 4 + j
            values = jnp.dot(held[leaf_ref[i]], wts[i], preferred_element_type=jnp.float32).T
            live = lax.broadcasted_iota(jnp.int32, values.shape, 0) < count_ref[i]
            start = pl.multiple_of(i * ROWS, ROWS)
            out_ref[pl.ds(start, ROWS), :] = jnp.where(live, values, 0.0).astype(jnp.bfloat16)

    @pl.loop(0, ly)
    def _(t):
        for step in range(1, groups):
            forward(t, step).wait_send()
            back(t, step).wait_send()
        to_core(t).wait_send()

    @when(gy > 0)
    def _():
        halo(False).wait_send()

    @when(gy < ny - 1)
    def _():
        halo(True).wait_send()

    if nz > 2:
        @when(gz < nz - 2)
        def _():
            halo_z(True).wait_send()

        @when(gz > 1)
        def _():
            halo_z(False).wait_send()


def local(sizes, coefficients, level_weights, coupling, positions, block_leaf, block_count):
    nx, ny, nz = sizes
    lx, ly, lz, cheb, cols = coefficients.shape
    groups = 2 * nx
    rows = cols // groups
    bf = jnp.bfloat16
    plane = (nx * lx, 2 * lz, rows, cheb)
    dma = pltpu.SemaphoreType.DMA
    anywhere = pl.BlockSpec(memory_space=pl.ANY)
    vmem = pl.BlockSpec(memory_space=pltpu.VMEM)
    smem = pl.BlockSpec(memory_space=pltpu.SMEM)
    return pl.pallas_call(
        functools.partial(grid_kernel, sizes),
        out_shape=jax.ShapeDtypeStruct((positions.shape[1], cols), bf),
        in_specs=[smem, smem, vmem, vmem, anywhere, anywhere],
        out_specs=vmem,
        scratch_shapes=[
            pltpu.VMEM(level_weights.shape, bf),
            pltpu.VMEM(coupling.shape, bf),
            pltpu.VMEM((groups, ly, lx, lz, rows, cheb), bf),
            pltpu.VMEM((ly,) + plane, bf),
            pltpu.VMEM((ly,) + plane, bf),
            pltpu.VMEM((ly,) + plane, bf),
            pltpu.VMEM((ly + 2, nx * lx + 2, 2 * lz + 2, rows, cheb), bf),
            pltpu.VMEM((ly,) + plane, bf),
            pltpu.VMEM((groups, ly, lx, lz, rows, cheb), bf),
            pltpu.VMEM((lx * ly * lz, cols, cheb), bf),
            pltpu.VMEM((block_leaf.shape[0], cheb, ROWS), bf),
            dma((4,)), dma,
            dma((groups, ly)), dma((groups, ly)),
            dma((ly,)), dma((ly,)),
            dma((2,)), dma((2,)), dma((2,)), dma((2,)),
            dma((groups, ly)), dma((groups, ly)),
        ],
        compiler_params=pltpu.CompilerParams(
            collective_id=0, has_side_effects=True, vmem_limit_bytes=58 << 20
        ),
    )(block_leaf, block_count, coefficients, positions, level_weights, coupling)


def solution(mesh):
    sizes = (mesh.shape["gx"], mesh.shape["gy"], mesh.shape["gz"])
    placed = (
        P("gx", "gy", "gz", None, None),
        P(),
        P(),
        P(None, ("gx", "gy", "gz")),
        P(("gx", "gy", "gz")),
        P(("gx", "gy", "gz")),
    )
    return jax.shard_map(
        functools.partial(local, sizes), mesh=mesh, in_specs=placed,
        out_specs=P(("gx", "gy", "gz"), None), check_vma=False,
    )
```

time: 131 us -> 113 us (0.86)
  Pallas kernels: 129 us -> 110 us
  local copies, waits for them, and re-layouts: 1.6 us -> 3.05 us
    pallas_call x2 -> x1, Pallas kernels: 129 us -> 110 us  [local(): pl.pallas_call(functools.partial(grid_kernel, sizes), out_shape=jax.Shape...]
    unnamed x8 -> x1, local copies, waits for them, and re-layouts: 1.6 us -> 3.05 us
where the time goes in v1:
time: 113 us
  Pallas kernels  110 us (97%)
  local copies, waits for them, and re-layouts  3.05 us (3%)
    pallas_call x1, Pallas kernels, local(): pl.pallas_call(functools.partial(grid_kernel, sizes), out_shape=jax.Shape...  110 us
    unnamed x1, local copies, waits for them, and re-layouts  3.05 us

profile of v1, /device:TPU:30, one launch (start us, length us, event | category | flops | bytes accessed | tf_op | source)
XLA Modules:
  0.0 112.8 jit_solution(4269523171206379781)
XLA Ops:
  0.0 109.7 %shard_map.64 = bf16[8192,128]{1,0:T(8,128)(2,1)} custom-call(s32[64]{0:T(128)} %leaf_ref.1, s32[64]{0:T(128)} %count_ref.1, bf16[2,4,2,512,128]{4,3,2,1,0:T(8,128)(2,1)} %x_ref.1, f32[3,8192]{1,0:T(4,128)} %pos_ref.1, bf16[4,2,2,512,512]{4,3,2,1,0:T(8,128)(2,1)} %w_hbm.1, bf16[6,512,512]{2,1,0:T(8,128)(2,1)} %k_hbm.1), custom_call_target="tpu_custom_call" | custom-call | tf_op jit(solution)/shard_map/pallas_call | solution.py:353
  109.7 3.0 %copy.8 = bf16[8192,128]{1,0:T(8,128)(2,1)} copy(bf16[8192,128]{1,0:T(8,128)(2,1)} %shard_map.64) | data formatting | bytes 4194304

commit v2 on v1

--- a/solution.py
+++ b/solution.py
@@ -34,7 +34,7 @@
 
 
 def grid_kernel(sizes, leaf_ref, count_ref, x_ref, pos_ref, w_hbm, k_hbm, out_ref,
-                w_ref, k_ref, src, xin, mid, got, pad, res, home, held, wts,
+                w_ref, k_ref, src, xin, mid, got, pad, res, home, held, wts, part,
                 w_sem, k_sem, fs_sem, fr_sem, ms_sem, mr_sem, hs_sem, hr_sem, zs_sem, zr_sem, bs_sem, br_sem):
     nx, ny, nz = sizes
     lx, ly, lz = x_ref.shape[:3]
@@ -45,6 +45,7 @@
     base = gz - bit
     me = gx * 2 + bit
     wide_x, wide_z = nx * lx, 2 * lz
+    order = sorted(range(1, groups), key=lambda step: abs(step - groups // 2))
 
     def peer(step):
         other = lax.rem(me + step, groups)
@@ -118,7 +119,7 @@
         @when(t > 0)
         def _():
             turn(t)
-        for step in range(1, groups):
+        for step in order:
             forward(t, step).start()
 
     pad[:, 0] = jnp.zeros_like(pad[:, 0])
@@ -199,19 +200,22 @@
             device_id=(px, gy, base + pz), device_id_type=MESH,
         )
 
-    def couple(y):
+    def terms(y, total, dirs):
         xs, zs = pl.ds(1, wide_x), pl.ds(1, wide_z)
-        here = pad[y + 1, xs, zs]
-        total = flat(here).astype(jnp.float32)
         places = (
             (y + 1, pl.ds(0, wide_x), zs), (y + 1, pl.ds(2, wide_x), zs),
             (y, xs, zs), (y + 2, xs, zs),
             (y + 1, xs, pl.ds(0, wide_z)), (y + 1, xs, pl.ds(2, wide_z)),
         )
-        for d, place in enumerate(places):
-            total = total + lax.dot_general(flat(pad[place]), k_ref[d], NT, preferred_element_type=jnp.float32)
-        res[y] = total.astype(jnp.bfloat16).reshape(here.shape)
-        for step in range(1, groups):
+        if total is None:
+            total = flat(pad[y + 1, xs, zs]).astype(jnp.float32)
+        for d in dirs:
+            total = total + lax.dot_general(flat(pad[places[d]]), k_ref[d], NT, preferred_element_type=jnp.float32)
+        return total
+
+    def couple(y, total=None, dirs=range(6)):
+        res[y] = terms(y, total, dirs).astype(jnp.bfloat16).reshape(res.shape[1:])
+        for step in order:
             back(y, step).start()
         home[me, y] = res[y, pl.ds(gx * lx, lx), pl.ds(bit * lz, lz)]
 
@@ -222,7 +226,12 @@
         def _():
             halo(False).wait_recv()
 
-    early = nz == 2
+    def from_below():
+        @when(gy > 0)
+        def _():
+            halo(True).wait_recv()
+
+    early = nz == 2 and ly == 4
 
     @pl.loop(0, ly + 1)
     def _(t):
@@ -246,6 +255,9 @@
             def _():
                 from_above()
                 couple(ly - 1)
+                part[0] = terms(2, None, (0, 1, 3, 4, 5))
+                from_below()
+                part[1] = terms(0, None, (0, 1, 2, 4, 5))
 
         @when(t < ly)
         def _():
@@ -274,16 +286,17 @@
         def _():
             halo_z(False).wait_recv()
 
-    if not early:
+    if early:
+        couple(2, part[0], (2,))
+        couple(0, part[1], (3,))
+        couple(1)
+    else:
         from_above()
-
-    @when(gy > 0)
-    def _():
-        halo(True).wait_recv()
-
-    @pl.loop(1 if early else 0, ly)
-    def _(t):
-        couple(ly - 1 - t)
+        from_below()
+
+        @pl.loop(0, ly)
+        def _(t):
+            couple(ly - 1 - t)
 
     @pl.loop(0, leaf_ref.shape[0])
     def _(i):
@@ -297,6 +310,9 @@
     @pl.loop(0, ly)
     def _(t):
         y = ly - 1 - t
+        if early:
+            late = lax.div(t, 2)
+            y = late * (t - 2) + (1 - late) * y
         for step in range(1, groups):
             back(y, step).wait_recv()
         for a in range(lx):
@@ -367,6 +383,7 @@
             pltpu.VMEM((groups, ly, lx, lz, rows, cheb), bf),
             pltpu.VMEM((lx * ly * lz, cols, cheb), bf),
             pltpu.VMEM((block_leaf.shape[0], cheb, ROWS), bf),
+            pltpu.VMEM((2, nx * lx * 2 * lz * rows, cheb), jnp.float32),
             dma((4,)), dma,
             dma((groups, ly)), dma((groups, ly)),
             dma((ly,)), dma((ly,)),

time: 113 us -> 113 us (level)
  the two profiles are of different devices: /device:TPU:30 before, /device:TPU:0 now
where the time goes in v2:
time: 113 us
  Pallas kernels  110 us (97%)
  local copies, waits for them, and re-layouts  3.05 us (3%)
    pallas_call x1, Pallas kernels, local(): pl.pallas_call(functools.partial(grid_kernel, sizes), out_shape=jax.Shape...  110 us
    unnamed x1, local copies, waits for them, and re-layouts  3.05 us

profile of v2, /device:TPU:0, one launch (start us, length us, event | category | flops | bytes accessed | tf_op | source)
XLA Modules:
  0.0 112.9 jit_solution(14291187634465687624)
XLA Ops:
  0.0 109.8 %shard_map.64 = bf16[8192,128]{1,0:T(8,128)(2,1)} custom-call(s32[64]{0:T(128)} %leaf_ref.1, s32[64]{0:T(128)} %count_ref.1, bf16[2,4,2,512,128]{4,3,2,1,0:T(8,128)(2,1)} %x_ref.1, f32[3,8192]{1,0:T(4,128)} %pos_ref.1, bf16[4,2,2,512,512]{4,3,2,1,0:T(8,128)(2,1)} %w_hbm.1, bf16[6,512,512]{2,1,0:T(8,128)(2,1)} %k_hbm.1), custom_call_target="tpu_custom_call" | custom-call | tf_op jit(solution)/shard_map/pallas_call | solution.py:369
  109.8 3.0 %copy.8 = bf16[8192,128]{1,0:T(8,128)(2,1)} copy(bf16[8192,128]{1,0:T(8,128)(2,1)} %shard_map.64) | data formatting | bytes 4194304
